TPU v7x, 32 devices: a whole 2x2x4 slice. The times are simulated.
32 devices in a mesh: group: 2 (over x), tm: 16 (over z, y, core).
Axes of the slice: x: 2, y: 2, z: 4, core: 2. Of those that a mesh axis runs over, the one named last changes fastest.
Arguments:
- obs_blocks: bfloat16 [32, 512, 64, 128], P(('group', 'tm')), parts along dimension 0, may hold values from -0.5 to 0.5
- block_rows: int32 [32, 512], P(('group', 'tm')), parts along dimension 0, may hold values from 0 to 511
- block_cols: int32 [32, 512], P(('group', 'tm')), parts along dimension 0, may hold values from 0 to 15
- block_count: int32 [32], P(('group', 'tm')), parts along dimension 0, may hold values from 256 to 512, as said below
- background: bfloat16 [32, 16, 2048], P(('group', 'tm')), parts along dimension 0, may hold values from -6 to 6
- observed: float32 [32, 16, 32768], P(('group', 'tm')), parts along dimension 0, may hold values from -6 to 6
- obs_weight: float32 [32, 32768], P(('group', 'tm')), parts along dimension 0, may hold values from 0.01 to 0.1
- info_diag: float32 [32, 2048], P(('group', 'tm')), parts along dimension 0, may hold values from 0.003 to 0.03
- decay: float32 [32, 2048], P(('group', 'tm')), parts along dimension 0, may hold values from 0.5 to 1
- noise_var: float32 [32, 2048], P(('group', 'tm')), parts along dimension 0, may hold values from 0.003 to 0.03
- prior_var: float32 [4096], P('group'), parts along dimension 0, may hold values from 0.5 to 2
Outputs:
- smooth_mean: float32 [32, 16, 2048], P(('group', 'tm')), parts along dimension 0
- smooth_var: float32 [32, 2048], P(('group', 'tm')), parts along dimension 0
There are 2 independent parts, one for each index of `group`. A program takes and returns all parts, laid end to end along the dimension named above; each array names one. Nothing has to cross between parts.
Inputs may be any that keep to these rules, and one draw needn't show every extreme that they name: Blocks 0 to block_count[t] - 1 of step t are in use; some step uses all 512 blocks and some step exactly half of them.
All inputs are finite; a program needn't handle non-finite values.
Results may differ from a plain program's by a relative error of at most 0.0045.
Values sent between devices are 32-bit elements; how exact they have to be, the bound alone decides.
A program may use at most 64 MiB of HBM per device.

v0:
```python
import jax
import jax.numpy as jnp
from jax import lax
from jax.sharding import PartitionSpec as P


def split_path(onehot, values, form):
    high_part = values.astype(jnp.bfloat16)
    rest_part = (values - high_part.astype(jnp.float32)).astype(jnp.bfloat16)
    first = jnp.einsum(form, onehot, high_part, preferred_element_type=jnp.float32)
    return first + jnp.einsum(form, onehot, rest_part, preferred_element_type=jnp.float32)


def gradients(obs_blocks, block_rows, block_cols, block_count, background, observed, obs_weight):
    step_total, block_total, row_size, col_size = obs_blocks.shape
    member_total = background.shape[1]
    group_total = background.shape[2] // col_size
    row_total = observed.shape[2] // row_size
    active = lax.broadcasted_iota(jnp.int32, (step_total, block_total), 1) < block_count[:, None]
    col_match = (
        block_cols[:, :, None]
        == lax.broadcasted_iota(jnp.int32, (step_total, block_total, group_total), 2)
    ).astype(jnp.bfloat16)
    row_match = block_rows[:, :, None] == lax.broadcasted_iota(
        jnp.int32, (step_total, block_total, row_total), 2
    )
    row_indicator = jnp.logical_and(row_match, active[:, :, None]).astype(jnp.bfloat16)
    states = background.reshape(step_total, member_total, group_total, col_size)
    picked = jnp.einsum(
        "sbk,smkc->smbc", col_match, states, preferred_element_type=jnp.float32
    ).astype(jnp.bfloat16)
    applied_result = jnp.einsum(
        "sbic,smbc->smbi", obs_blocks, picked, preferred_element_type=jnp.float32
    )
    mapped_images = split_path(row_indicator, applied_result, "dez,dwet->dwzt")
    misfit = observed - mapped_images.reshape(step_total, member_total, row_total * row_size)
    weighted = (obs_weight[:, None, :] * misfit).reshape(
        step_total, member_total, row_total, row_size
    )
    rows_back = jnp.einsum(
        "ocd,owdh->owch",
        row_indicator,
        weighted.astype(jnp.bfloat16),
        preferred_element_type=jnp.float32,
    ).astype(jnp.bfloat16)
    pulled = jnp.einsum(
        "sbic,smbi->smbc", obs_blocks, rows_back, preferred_element_type=jnp.float32
    )
    gradient = split_path(col_match, pulled, "sbk,smbc->smkc")
    return gradient.reshape(step_total, member_total, group_total * col_size)


def sequential_smoother(series, prior_here, member_total):
    full_steps = series.shape[0]
    grad_all = series[:, :member_total, :]
    info_all = series[:, member_total, :]
    decay_all = series[:, member_total + 1, :]
    noise_all = series[:, member_total + 2, :]
    local_width = series.shape[2]
    step_ids = jnp.arange(full_steps)
    first_flags = step_ids == 0
    final_flags = step_ids == full_steps - 1

    def forward(carried, inputs):
        mean_prev, var_prev = carried
        grad_now, info_now, decay_now, noise_now, first_now = inputs
        pred_var = jnp.where(first_now, prior_here, decay_now * decay_now * var_prev + noise_now)
        pred_mean = jnp.where(first_now, 0.0, decay_now * mean_prev)
        var_now = pred_var / (1.0 + info_now * pred_var)
        mean_now = var_now * (pred_mean / pred_var + grad_now)
        return ((mean_now, var_now), (mean_now, var_now))

    initial = (
        jnp.zeros((member_total, local_width), jnp.float32),
        jnp.ones((local_width,), jnp.float32),
    )
    means, variances = lax.scan(
        forward, initial, (grad_all, info_all, decay_all, noise_all, first_flags)
    )[1]
    next_decay = jnp.concatenate([decay_all[1:], jnp.zeros((1, local_width), jnp.float32)], axis=0)
    next_noise = jnp.concatenate([noise_all[1:], jnp.ones((1, local_width), jnp.float32)], axis=0)

    def backward(carried, inputs):
        later_mean, later_var = carried
        mean_now, var_now, decay_next, noise_next, final_now = inputs
        pred_var = decay_next * decay_next * var_now + noise_next
        smoother_gain = jnp.where(final_now, 0.0, var_now * decay_next / pred_var)
        out_mean = mean_now + smoother_gain * (later_mean - decay_next * mean_now)
        out_var = var_now + smoother_gain * smoother_gain * (later_var - pred_var)
        return ((out_mean, out_var), (out_mean, out_var))

    closing = (
        jnp.zeros((member_total, local_width), jnp.float32),
        jnp.zeros((local_width,), jnp.float32),
    )
    return lax.scan(
        backward, closing, (means, variances, next_decay, next_noise, final_flags), reverse=True
    )[1]


def shards(
    obs_blocks,
    block_rows,
    block_cols,
    block_count,
    background,
    observed,
    obs_weight,
    info_diag,
    decay,
    noise_var,
    prior_var,
):
    member_total = background.shape[1]
    state_total = background.shape[2]
    gradient = gradients(
        obs_blocks, block_rows, block_cols, block_count, background, observed, obs_weight
    )
    packed = jnp.concatenate(
        [gradient, info_diag[:, None, :], decay[:, None, :], noise_var[:, None, :]], axis=1
    )
    series = lax.all_to_all(packed, "tm", split_axis=2, concat_axis=0, tiled=True)
    local_width = state_total // lax.axis_size("tm")
    prior_here = lax.dynamic_slice_in_dim(
        prior_var, lax.axis_index("tm") * local_width, local_width, 0
    )
    mean_series, var_series = sequential_smoother(series, prior_here, member_total)
    outgoing = jnp.concatenate([mean_series, var_series[:, None, :]], axis=1)
    returned = lax.all_to_all(outgoing, "tm", split_axis=0, concat_axis=2, tiled=True)
    return (returned[:, :member_total, :], returned[:, member_total, :])


def solution(mesh):
    in_specs = (
        P(("group", "tm"), None, None, None),
        P(("group", "tm"), None),
        P(("group", "tm"), None),
        P(("group", "tm")),
        P(("group", "tm"), None, None),
        P(("group", "tm"), None, None),
        P(("group", "tm"), None),
        P(("group", "tm"), None),
        P(("group", "tm"), None),
        P(("group", "tm"), None),
        P("group"),
    )
    out_specs = (P(("group", "tm"), None, None), P(("group", "tm"), None))
    return jax.shard_map(shards, mesh=mesh, in_specs=in_specs, out_specs=out_specs, check_vma=False)
```

profile of v0, /device:TPU:0, one launch (start us, length us, event | category | flops | bytes accessed | tf_op | source)
XLA Modules:
  0.0 153.4 jit_solution(15889140871200153109)
XLA Ops:
  0.6 0.9 copy.100
  1.5 1.4 convert_bitcast_fusion
  2.9 7.2 %fusion.23 = f32[512,16,64]{2,1,0:T(8,128)S(1)} fusion(bf16[1,512,64,128]{3,2,1,0:T(8,128)(2,1)} %param.15, bf16[16,512,128]{2,1,0:T(8,128)(2,1)S(1)} %convert_bitcast_fusion), kind=kOutput, calls=%fused_computation.44 | convolution fusion | flops 134217728 | bytes 12582912 | tf_op jit(solution)/shard_map/sbic,smbc->smbi/dot_general | solution.py:32
  11.5 1.0 fusion.33
  12.5 1.1 add_bitcast_fusion
  13.6 2.7 %copy.84 = f32[1,16,512,64]{3,2,1,0:T(8,128)} copy(f32[1,16,512,64]{2,3,1,0:T(8,128)S(1)} %add_bitcast_fusion) | data formatting | bytes 4194304 | tf_op jit(solution)/shard_map/add | solution.py:11
  16.3 2.9 %reshape.249 = f32[1,16,32768]{2,1,0:T(8,128)S(1)} reshape(f32[1,16,512,64]{3,2,1,0:T(8,128)} %copy.84) | data formatting | bytes 4194304 | tf_op jit(solution)/shard_map/reshape | solution.py:36
  19.3 1.8 %multiply_convert_fusion = bf16[1,16,32768]{2,1,0:T(8,128)(2,1)S(1)} fusion(f32[1,16,32768]{2,1,0:T(8,128)} %param.20, f32[1,16,32768]{2,1,0:T(8,128)S(1)} %reshape.249, f32[32768]{0:T(1024)S(1)} %bitcast.211), kind=kLoop, calls=%fused_computation.63 | loop fusion | flops 1572864 | bytes 5373952 | tf_op jit(solution)/shard_map/convert_element_type | solution.py:43
  21.1 2.3 %convert_element_type.58 = bf16[16,512,64]{2,1,0:T(8,128)(2,1)S(1)} reshape(bf16[1,16,32768]{2,1,0:T(8,128)(2,1)S(1)} %multiply_convert_fusion) | data formatting | bytes 2097152 | tf_op jit(solution)/shard_map/convert_element_type | solution.py:43
  23.4 1.5 fusion.40
  24.9 2.0 %copy.86 = bf16[16,512,64]{2,0,1:T(8,128)(2,1)S(1)} copy(bf16[16,512,64]{1,2,0:T(8,128)(2,1)S(1)} %fusion.40) | data formatting | bytes 2097152 | tf_op jit(solution)/shard_map/reshape.26
  26.9 4.7 %fusion.21 = f32[512,16,128]{2,1,0:T(8,128)S(1)} fusion(bf16[16,512,64]{2,0,1:T(8,128)(2,1)S(1)} %copy.86, bf16[1,512,64,128]{3,2,1,0:T(8,128)(2,1)} %param.15), kind=kOutput, calls=%fused_computation.42 | convolution fusion | flops 134217728 | bytes 13631488 | tf_op jit(solution)/shard_map/sbic,smbi->smbc/dot_general | solution.py:46
  34.4 1.9 %copy.91 = f32[1,1,2048]{1,0,2:T(1,128)} copy(f32[1,1,2048]{2,1,0:T(1,128)S(1)} %bitcast.217) | data formatting | bytes 16384 | tf_op jit(solution)/shard_map/broadcast_in_dim | solution.py:120
  36.3 1.9 %copy.92 = f32[1,1,2048]{1,0,2:T(1,128)} copy(f32[1,1,2048]{2,1,0:T(1,128)S(1)} %bitcast.218) | data formatting | bytes 16384 | tf_op jit(solution)/shard_map/broadcast_in_dim | solution.py:120
  38.2 7.8 %fusion.69 = f32[2048,1,19]{2,1,0:T(1,128)S(1)} fusion(f32[1,1,2048]{1,0,2:T(1,128)} %copy.92, f32[1,1,2048]{1,0,2:T(1,128)} %copy.91, f32[1,1,2048]{1,0,2:T(1,128)S(1)} %copy.90, f32[1,16,2048]{1,0,2:T(1,128)S(1)} %bitcast.203), kind=kLoop, calls=%fused_computation.97 | loop fusion | flops 116736 | bytes 311296
  46.6 9.3 %reduce = f32[2048,19]{1,0:T(8,128)S(1)} reduce(f32[2048,1,19]{2,1,0:T(1,128)S(1)} %fusion.69, f32[]{:T(128)} %broadcast.158), dimensions={1}, to_apply=%fusion.69.reduce_sub_computation | reduce | bytes 311300
  55.8 1.5 reshape.256
  57.4 7.4 %all-to-all-start = ((f32[16,1,2432]{2,1,0:T(1,128)}), f32[16,1,2432]{2,1,0:T(1,128)S(1)}, u32[]{:S(2)}, u32[]{:S(2)}) async-start(f32[16,1,2432]{2,1,0:T(1,128)} %reshape.256), calls=%async_computation | async-start | bytes 311296 | tf_op jit(solution)/shard_map/all_to_all | solution.py:122
  65.6 7.5 %all-to-all-done = f32[16,1,2432]{2,1,0:T(1,128)S(1)} async-done(((f32[16,1,2432]{2,1,0:T(1,128)}), f32[16,1,2432]{2,1,0:T(1,128)S(1)}, u32[]{:S(2)}, u32[]{:S(2)}) %all-to-all-start) | async-done | bytes 155680 | tf_op jit(solution)/shard_map/all_to_all | solution.py:122
  73.1 0.9 reduce.1
  74.0 1.7 %reshape.257 = f32[2048,1,19]{2,1,0:T(1,128)S(1)} reshape(f32[16,2432]{1,0:T(8,128)S(1)} %reduce.1) | data formatting | bytes 311296
  76.4 31.9 %while.38 = (s32[]{:T(128)}, f32[16,128]{1,0:T(8,128)S(1)}, f32[128]{0:T(128)S(1)}, f32[16,16,128]{2,1,0:T(8,128)S(1)}, f32[16,128]{1,0:T(8,128)S(1)}, /*index=5...) while((s32[]{:T(128)}, f32[16,128]{1,0:T(8,128)S(1)}, ...), condition=%wide.region_1.2_spmd.clone, body=%wide.region_0.1_spmd.clone.sunk | while | flops 13315 | bytes 55968 | solution.py:77
  108.3 32.1 %while.39 = (s32[]{:T(128)}, f32[16,128]{1,0:T(8,128)S(1)}, f32[128]{0:T(128)S(1)}, f32[16,16,128]{2,1,0:T(8,128)S(1)}, f32[16,128]{1,0:T(8,128)S(1)}, /*index=5...) while((s32[]{:T(128)}, f32[16,128]{1,0:T(8,128)S(1)}, ...), condition=%wide.region_3.4_spmd.clone, body=%wide.region_2.3_spmd.clone.sunk | while | flops 12420 | bytes 40108 | solution.py:96
  140.4 11.6 %all_to_all.36 = f32[16,17,128]{2,1,0:T(8,128)S(1)} all-to-all(f32[16,17,128]{2,1,0:T(8,128)S(1)} %pad_maximum_fusion.1), channel_id=1, replica_groups=mesh['group'=2,'tm'=16] {'tm'}, dimensions={0} | all-to-all | bytes 278528 | tf_op jit(solution)/shard_map/all_to_all | solution.py:129
  (204 shorter events, 69.6 us)
Async XLA Ops:
  10.5 1.0 copy-start.4
  16.3 3.0 %copy-start = (f32[1,32768]{1,0:T(1,128)S(1)}, f32[1,32768]{1,0:T(1,128)}, u32[]{:S(2)}) copy-start(f32[1,32768]{1,0:T(1,128)} %param.21) | copy-start | bytes 393220
  31.9 0.7 copy-start.5
  33.0 0.8 copy-start.1
  33.0 1.4 copy-start.2
  33.4 2.9 %copy-start.3 = (f32[1,2048]{1,0:T(1,128)S(1)}, f32[1,2048]{1,0:T(1,128)}, u32[]{:S(2)}) copy-start(f32[1,2048]{1,0:T(1,128)} %param.24) | copy-start | bytes 24580
  57.4 15.7 %all-to-all-start = ((f32[16,1,2432]{2,1,0:T(1,128)}), f32[16,1,2432]{2,1,0:T(1,128)S(1)}, u32[]{:S(2)}, u32[]{:S(2)}) async-start(f32[16,1,2432]{2,1,0:T(1,128)} %reshape.256), calls=%async_computation | async-start | bytes 311296 | tf_op jit(solution)/shard_map/all_to_all | solution.py:122
where the time goes:
time: 154 us; the launch traced here: 153 us
  other arithmetic  63.4 us (41%)
  local copies, waits for them, and re-layouts  43.1 us (28%)
  matrix products  17.7 us (11%)
  blocking collectives  11.6 us (8%)
  waiting for transfers between devices  7.51 us (5%)
  starting transfers between devices  7.39 us (5%)
  between operations  1.64 us (1%)
    dynamic_slice x48, local copies, waits for them, and re-layouts, sequential_smoother(): lax.scan(forward, initial, (grad_all, info_all, decay_all, noise_all, fir...  19.5 us
    unnamed x6, other arithmetic  17.1 us
    all_to_all x1, blocking collectives, shards(): lax.all_to_all(outgoing, 'tm', split_axis=0, concat_axis=2, tiled=True)  11.6 us
    add x16, other arithmetic, backward(): out_var = var_now + smoother_gain * smoother_gain * (later_var - pred_var)  10.7 us
    mul x16, other arithmetic, backward(): out_mean = mean_now + smoother_gain * (later_mean - decay_next * mean_now)  10.5 us
    dynamic_update_slice x32, other arithmetic, sequential_smoother(): lax.scan(forward, initial, (grad_all, info_all, decay_all, noise_all, fir...  10.5 us
    div x16, other arithmetic, forward(): var_now = pred_var / (1.0 + info_now * pred_var)  10.5 us
    all_to_all x1, waiting for transfers between devices, shards(): lax.all_to_all(packed, 'tm', split_axis=2, concat_axis=0, tiled=True)  7.51 us
  transfers between devices with their start and end apart: 1, of which 1 were waited for; matrix products, arithmetic and copies ran while one was open for 1% of the time, Pallas kernels for 0%

commit v1 on v0

--- a/solution.py
+++ b/solution.py
@@ -1,53 +1,269 @@
+import functools
+
 import jax
 import jax.numpy as jnp
 from jax import lax
+from jax.experimental import pallas as pl
+from jax.experimental.pallas import tpu as pltpu
 from jax.sharding import PartitionSpec as P
 
-
-def split_path(onehot, values, form):
-    high_part = values.astype(jnp.bfloat16)
-    rest_part = (values - high_part.astype(jnp.float32)).astype(jnp.bfloat16)
-    first = jnp.einsum(form, onehot, high_part, preferred_element_type=jnp.float32)
-    return first + jnp.einsum(form, onehot, rest_part, preferred_element_type=jnp.float32)
+MESH = pl.DeviceIdType.MESH
+CHUNKS = 8
+GROUP = 4
+
+
+def gradient_kernel(
+    rows, cols, count, back_ref, weight_ref, blocks_hbm, observed_hbm,
+    out_ref, states, blocks, misfit, block_sems, observed_sem,
+):
+    block_total = rows.shape[1]
+    row_size = blocks.shape[0] // block_total
+    members = back_ref.shape[1]
+    state_total, _, col_size = states.shape
+    chunk = block_total // CHUNKS
+
+    observed_copy = pltpu.make_async_copy(observed_hbm, misfit, observed_sem)
+    observed_copy.start()
+    copies = []
+    for part in range(CHUNKS):
+        span = pl.ds(part * chunk * row_size, chunk * row_size)
+        copies.append(
+            pltpu.make_async_copy(blocks_hbm.at[span], blocks.at[span], block_sems.at[part])
+        )
+        copies[-1].start()
+
+    for k in range(state_total):
+        states[k] = back_ref[0, :, k * col_size:(k + 1) * col_size]
+    out_ref[...] = jnp.zeros_like(out_ref)
+    lane_half = lax.broadcasted_iota(jnp.int32, (members, 2 * row_size), 1) // row_size
+    in_use = count[0]
+    observed_copy.wait()
+
+    def place(row):
+        return pl.ds(pl.multiple_of((row // 2) * 2 * row_size, 2 * row_size), 2 * row_size)
+
+    def apply_group(group, _):
+        first = group * GROUP
+        picked = jnp.concatenate([states[cols[0, first + j]] for j in range(GROUP)], axis=0)
+        tile = blocks[pl.ds(pl.multiple_of(first * row_size, GROUP * row_size), GROUP * row_size), :]
+        applied = lax.dot_general(
+            picked, tile, (((1,), (1,)), ((), ())), preferred_element_type=jnp.float32
+        )
+        for j in range(GROUP):
+            row = rows[0, first + j]
+            half = row % 2
+            piece = applied[
+                j * members:(j + 1) * members,
+                (j // 2) * 2 * row_size:(j // 2 + 1) * 2 * row_size,
+            ]
+            piece = pltpu.roll(piece, (half ^ (j % 2)) * row_size, 1)
+            wanted = jnp.where(first + j < in_use, half, 2)
+            at = place(row)
+            misfit[:, at] = misfit[:, at] - jnp.where(lane_half == wanted, piece, 0.0)
+        return 0
+
+    for part in range(CHUNKS):
+        copies[part].wait()
+        per = chunk // GROUP
+        lax.fori_loop(part * per, (part + 1) * per, apply_group, 0, unroll=4)
+
+    def pull_group(group, _):
+        first = group * GROUP
+        pieces = []
+        for j in range(GROUP):
+            row = rows[0, first + j]
+            at = place(row)
+            value = misfit[:, at] * weight_ref[:, at]
+            value = pltpu.roll(value, ((row % 2) ^ (j % 2)) * row_size, 1)
+            wanted = jnp.where(first + j < in_use, j % 2, 2)
+            value = jnp.where(lane_half == wanted, value, 0.0).astype(jnp.bfloat16)
+            nothing = jnp.zeros_like(value)
+            pieces.append(
+                jnp.concatenate([value if s == j // 2 else nothing for s in range(GROUP // 2)], axis=1)
+            )
+        tile = blocks[pl.ds(pl.multiple_of(first * row_size, GROUP * row_size), GROUP * row_size), :]
+        pulled = jnp.dot(
+            jnp.concatenate(pieces, axis=0), tile, preferred_element_type=jnp.float32
+        )
+        for j in range(GROUP):
+            k = cols[0, first + j]
+            out_ref[k] = out_ref[k] + pulled[j * members:(j + 1) * members]
+        return 0
+
+    lax.fori_loop(0, block_total // GROUP, pull_group, 0, unroll=4)
 
 
 def gradients(obs_blocks, block_rows, block_cols, block_count, background, observed, obs_weight):
-    step_total, block_total, row_size, col_size = obs_blocks.shape
-    member_total = background.shape[1]
-    group_total = background.shape[2] // col_size
-    row_total = observed.shape[2] // row_size
-    active = lax.broadcasted_iota(jnp.int32, (step_total, block_total), 1) < block_count[:, None]
-    col_match = (
-        block_cols[:, :, None]
-        == lax.broadcasted_iota(jnp.int32, (step_total, block_total, group_total), 2)
-    ).astype(jnp.bfloat16)
-    row_match = block_rows[:, :, None] == lax.broadcasted_iota(
-        jnp.int32, (step_total, block_total, row_total), 2
-    )
-    row_indicator = jnp.logical_and(row_match, active[:, :, None]).astype(jnp.bfloat16)
-    states = background.reshape(step_total, member_total, group_total, col_size)
-    picked = jnp.einsum(
-        "sbk,smkc->smbc", col_match, states, preferred_element_type=jnp.float32
-    ).astype(jnp.bfloat16)
-    applied_result = jnp.einsum(
-        "sbic,smbc->smbi", obs_blocks, picked, preferred_element_type=jnp.float32
-    )
-    mapped_images = split_path(row_indicator, applied_result, "dez,dwet->dwzt")
-    misfit = observed - mapped_images.reshape(step_total, member_total, row_total * row_size)
-    weighted = (obs_weight[:, None, :] * misfit).reshape(
-        step_total, member_total, row_total, row_size
-    )
-    rows_back = jnp.einsum(
-        "ocd,owdh->owch",
-        row_indicator,
-        weighted.astype(jnp.bfloat16),
-        preferred_element_type=jnp.float32,
-    ).astype(jnp.bfloat16)
-    pulled = jnp.einsum(
-        "sbic,smbi->smbc", obs_blocks, rows_back, preferred_element_type=jnp.float32
-    )
-    gradient = split_path(col_match, pulled, "sbk,smbc->smkc")
-    return gradient.reshape(step_total, member_total, group_total * col_size)
+    _, block_total, row_size, col_size = obs_blocks.shape
+    members = background.shape[1]
+    state_total = background.shape[2] // col_size
+    smem = pl.BlockSpec(memory_space=pltpu.SMEM)
+    vmem = pl.BlockSpec(memory_space=pltpu.VMEM)
+    hbm = pl.BlockSpec(memory_space=pltpu.HBM)
+    return pl.pallas_call(
+        gradient_kernel,
+        out_shape=jax.ShapeDtypeStruct((state_total, members, col_size), jnp.float32),
+        in_specs=[smem, smem, smem, vmem, vmem, hbm, hbm],
+        out_specs=vmem,
+        scratch_shapes=[
+            pltpu.VMEM((state_total, members, col_size), jnp.bfloat16),
+            pltpu.VMEM((block_total * row_size, col_size), jnp.bfloat16),
+            pltpu.VMEM((members, observed.shape[2]), jnp.float32),
+            pltpu.SemaphoreType.DMA((CHUNKS,)),
+            pltpu.SemaphoreType.DMA,
+        ],
+        compiler_params=pltpu.CompilerParams(vmem_limit_bytes=62 * 2**20),
+        name="local_gradient",
+    )(
+        block_rows, block_cols, block_count, background, obs_weight,
+        obs_blocks.reshape(block_total * row_size, col_size),
+        observed.reshape(members, observed.shape[2]),
+    )
+
+
+def smoother_kernel(
+    n, grad_ref, info_ref, decay_ref, noise_ref, prior_ref, mean_out, var_out,
+    coef_send, coef_recv, grad_recv, mean_send, var_send,
+    coef_ss, coef_rs, grad_ss, grad_rs, mean_ss, mean_rs, var_ss, var_rs,
+):
+    me = lax.axis_index("tm")
+    width = coef_send.shape[2]
+
+    barrier = pltpu.get_barrier_semaphore()
+
+    def greet(d, _):
+        pl.semaphore_signal(
+            barrier, inc=1, device_id={"tm": lax.rem(me + d, n)}, device_id_type=MESH
+        )
+        return 0
+
+    lax.fori_loop(1, n, greet, 0)
+    for k in range(n):
+        columns = slice(k * width, (k + 1) * width)
+        coef_send[k, 0:1, :] = info_ref[:, columns]
+        coef_send[k, 1:2, :] = decay_ref[:, columns]
+        coef_send[k, 2:3, :] = noise_ref[:, columns]
+    mine = pl.ds(pl.multiple_of(me * width, width), width)
+    coef_recv[me] = coef_send[me]
+    grad_recv[me] = grad_ref[me]
+    pl.semaphore_wait(barrier, n - 1)
+
+    def remote(src, dst, send_sem, recv_sem, d):
+        to = lax.rem(me + d, n)
+        return pltpu.make_async_remote_copy(
+            src_ref=src(to), dst_ref=dst(me), send_sem=send_sem.at[to], recv_sem=recv_sem.at[me],
+            device_id={"tm": to}, device_id_type=MESH,
+        )
+
+    def arrival(src, dst, send_sem, recv_sem, d):
+        other = lax.rem(me + d, n)
+        return pltpu.make_async_remote_copy(
+            src_ref=src(other), dst_ref=dst(other), send_sem=send_sem.at[other],
+            recv_sem=recv_sem.at[other], device_id={"tm": other}, device_id_type=MESH,
+        )
+
+    def start_all(*what):
+        def body(d, _):
+            remote(*what, d).start()
+            return 0
+        lax.fori_loop(1, n, body, 0)
+
+    def wait_all(*what):
+        def body(d, _):
+            arrival(*what, d).wait_recv()
+            return 0
+        lax.fori_loop(1, n, body, 0)
+
+    def sent_all(*what):
+        def body(d, _):
+            remote(*what, d).wait_send()
+            return 0
+        lax.fori_loop(1, n, body, 0)
+
+    def columns_of(ref):
+        return lambda k: ref.at[:, pl.ds(pl.multiple_of(k * width, width), width)]
+
+    coefs = (lambda k: coef_send.at[k], lambda k: coef_recv.at[k], coef_ss, coef_rs)
+    grads = (lambda k: grad_ref.at[k], lambda k: grad_recv.at[k], grad_ss, grad_rs)
+    means = (lambda k: mean_send.at[k], columns_of(mean_out), mean_ss, mean_rs)
+    varis = (lambda k: var_send.at[k], columns_of(var_out), var_ss, var_rs)
+
+    start_all(*coefs)
+    start_all(*grads)
+    wait_all(*coefs)
+
+    info = [coef_recv[t, 0:1, :] for t in range(n)]
+    decay = [coef_recv[t, 1:2, :] for t in range(n)]
+    noise = [coef_recv[t, 2:3, :] for t in range(n)]
+    var, carry = [], []
+    for t in range(n):
+        if t == 0:
+            pred = prior_ref[:, mine]
+            carry.append(None)
+        else:
+            pred = decay[t] * decay[t] * var[t - 1] + noise[t]
+        scale = 1.0 / (1.0 + info[t] * pred)
+        var.append(pred * scale)
+        if t > 0:
+            carry.append(scale * decay[t])
+    gain = []
+    later = [None] * n
+    later[n - 1] = var[n - 1]
+    for t in range(n - 1):
+        pred = decay[t + 1] * decay[t + 1] * var[t] + noise[t + 1]
+        gain.append(var[t] * decay[t + 1] / pred)
+    for t in range(n - 2, -1, -1):
+        pred = decay[t + 1] * decay[t + 1] * var[t] + noise[t + 1]
+        later[t] = var[t] + gain[t] * gain[t] * (later[t + 1] - pred)
+    for t in range(n):
+        var_send[t] = later[t]
+    start_all(*varis)
+    var_out[:, mine] = var_send[me]
+
+    wait_all(*grads)
+    mean = []
+    for t in range(n):
+        now = var[t] * grad_recv[t]
+        mean.append(now if t == 0 else carry[t] * mean[t - 1] + now)
+    smooth = mean[n - 1]
+    mean_send[n - 1] = smooth
+    for t in range(n - 2, -1, -1):
+        smooth = mean[t] + gain[t] * (smooth - decay[t + 1] * mean[t])
+        mean_send[t] = smooth
+    start_all(*means)
+    mean_out[:, mine] = mean_send[me]
+
+    wait_all(*varis)
+    wait_all(*means)
+    sent_all(*coefs)
+    sent_all(*grads)
+    sent_all(*varis)
+    sent_all(*means)
+
+
+def exchange_and_smooth(n, gradient, info_diag, decay, noise_var, prior_var):
+    state_total, members, width = gradient.shape
+    total = state_total * width
+    vmem = pl.BlockSpec(memory_space=pltpu.VMEM)
+    mean, var = pl.pallas_call(
+        functools.partial(smoother_kernel, n),
+        out_shape=(
+            jax.ShapeDtypeStruct((members, total), jnp.float32),
+            jax.ShapeDtypeStruct((1, total), jnp.float32),
+        ),
+        in_specs=[vmem] * 5,
+        out_specs=(vmem, vmem),
+        scratch_shapes=[
+            pltpu.VMEM((n, 3, width), jnp.float32),
+            pltpu.VMEM((n, 3, width), jnp.float32),
+            pltpu.VMEM((n, members, width), jnp.float32),
+            pltpu.VMEM((n, members, width), jnp.float32),
+            pltpu.VMEM((n, 1, width), jnp.float32),
+        ] + [pltpu.SemaphoreType.DMA((n,))] * 8,
+        compiler_params=pltpu.CompilerParams(collective_id=0, has_side_effects=True),
+        name="exchange_smooth",
+    )(gradient, info_diag, decay, noise_var, prior_var.reshape(1, total))
+    return mean[None], var
 
 
 def sequential_smoother(series, prior_here, member_total):
@@ -113,14 +329,18 @@
 ):
     member_total = background.shape[1]
     state_total = background.shape[2]
+    n = lax.axis_size("tm")
     gradient = gradients(
         obs_blocks, block_rows, block_cols, block_count, background, observed, obs_weight
     )
+    local_width = state_total // n
+    if local_width == gradient.shape[2]:
+        return exchange_and_smooth(n, gradient, info_diag, decay, noise_var, prior_var)
+    gradient = jnp.transpose(gradient, (1, 0, 2)).reshape(1, member_total, state_total)
     packed = jnp.concatenate(
         [gradient, info_diag[:, None, :], decay[:, None, :], noise_var[:, None, :]], axis=1
     )
     series = lax.all_to_all(packed, "tm", split_axis=2, concat_axis=0, tiled=True)
-    local_width = state_total // lax.axis_size("tm")
     prior_here = lax.dynamic_slice_in_dim(
         prior_var, lax.axis_index("tm") * local_width, local_width, 0
     )

time: 154 us -> 48.9 us (0.32)
  other arithmetic: 63.4 us -> 0 us
  Pallas kernels: 0 us -> 44.5 us
  local copies, waits for them, and re-layouts: 43.1 us -> 2.86 us
  matrix products: 17.7 us -> 0 us
  blocking collectives: 11.6 us -> 0 us
  waiting for transfers between devices: 7.51 us -> 0 us
  starting transfers between devices: 7.39 us -> 0 us
    pallas_call x0 -> x2, Pallas kernels: none -> 44.5 us  [the longest x1 25.2 us: gradients(): pl.pallas_call(gradient_kernel, out_shape=jax.ShapeDtypeStruct((state_tot...]
    dynamic_slice x49 -> x0, local copies, waits for them, and re-layouts: 20.2 us -> none  [the longest x48 19.5 us: sequential_smoother(): lax.scan(forward, initial, (grad_all, info_all, decay_all, noise_all, fir...]
    dot_general x8 -> x0, matrix products: 17.7 us -> none  [the longest x1 7.23 us: gradients(): jnp.einsum('sbic,smbc->smbi', obs_blocks, picked, preferred_element_type=...]
    unnamed x6 -> x0, other arithmetic: 17.1 us -> none
    all_to_all x1 -> x0, blocking collectives: 11.6 us -> none  [shards(): lax.all_to_all(outgoing, 'tm', split_axis=0, concat_axis=2, tiled=True)]
    add x16 -> x0, other arithmetic: 10.7 us -> none  [backward(): out_var = var_now + smoother_gain * smoother_gain * (later_var - pred_var)]
    mul x16 -> x0, other arithmetic: 10.5 us -> none  [backward(): out_mean = mean_now + smoother_gain * (later_mean - decay_next * mean_now)]
    dynamic_update_slice x32 -> x0, other arithmetic: 10.5 us -> none  [sequential_smoother(): lax.scan(forward, initial, (grad_all, info_all, decay_all, noise_all, fir...]
  transfers between devices with their start and end apart: 1 -> 0, of which waited for: 1 -> 0; matrix products, arithmetic and copies ran while one was open for 1% -> 0% of each run, Pallas kernels for 0% -> 0%
where the time goes in v1:
time: 48.9 us; the launch traced here: 48.6 us
  Pallas kernels  44.5 us (91%)
  local copies, waits for them, and re-layouts  2.86 us (6%)
  between operations  1.29 us (3%)
    pallas_call x1, Pallas kernels, gradients(): pl.pallas_call(gradient_kernel, out_shape=jax.ShapeDtypeStruct((state_tot...  25.2 us
    pallas_call x1, Pallas kernels, exchange_and_smooth(): pl.pallas_call(functools.partial(smoother_kernel, n), out_shape=(jax.Shap...  19.3 us
    unnamed x2, local copies, waits for them, and re-layouts  2.86 us

profile of v1, /device:TPU:0, one launch (start us, length us, event | category | flops | bytes accessed | tf_op | source)
XLA Modules:
  0.0 48.6 jit_solution(6566122926140978510)
XLA Ops:
  1.3 25.2 %local_gradient.1.grad_ref = f32[16,16,128]{2,1,0:T(8,128)} custom-call(s32[1,512]{1,0:T(1,128)} %rows.1, s32[1,512]{1,0:T(1,128)} %cols.1, s32[1]{0:T(128)S(6)} %copy.15.count, bf16[1,16,2048]{2,1,0:T(8,128)(2,1)} %back_ref.1, f32[1,32768]{1,0:T(1,128)} %weight_ref.1, bf16[32768,128]{1,0:T(8,128)(2,1)} %bitcast.4, f32[16,32768]{1,0:T(8,128)} %bitcast.5), custom_call_target="tpu_custom_call" | custom-call | tf_op jit(solution)/shard_map/local_gradient/pallas_call | solution.py:103
  26.5 19.3 %exchange_smooth.1 = (f32[16,2048]{1,0:T(8,128)}, f32[1,2048]{1,0:T(1,128)}) custom-call(f32[16,16,128]{2,1,0:T(8,128)} %local_gradient.1.grad_ref, f32[1,2048]{1,0:T(1,128)} %info_ref.1, f32[1,2048]{1,0:T(1,128)} %decay_ref.1, f32[1,2048]{1,0:T(1,128)} %noise_ref.1, f32[1,2048]{1,0:T(1,128)} %bitcast.7), custom_call_target="tpu_custom_call" | custom-call | tf_op jit(solution)/shard_map/exchange_smooth/pallas_call | solution.py:248
  45.8 1.6 %copy.16 = f32[1,16,2048]{2,1,0:T(8,128)} copy(f32[1,16,2048]{2,1,0:T(8,128)} %bitcast.6) | data formatting | bytes 262144
  47.4 1.3 %copy.17 = f32[1,2048]{1,0:T(1,128)} copy(f32[1,2048]{1,0:T(1,128)} %get-tuple-element.9) | data formatting | bytes 16384

commit v2 on v1

v2 whole, which is shorter than its diff:
```python
import functools

import jax
import jax.numpy as jnp
from jax import lax
from jax.experimental import pallas as pl
from jax.experimental.pallas import tpu as pltpu
from jax.sharding import PartitionSpec as P

MESH = pl.DeviceIdType.MESH
CHUNKS = 2
GROUP = 4


def gradient_kernel(
    rows, cols, count, back_hbm, weight_hbm, blocks_hbm, observed_hbm,
    out_ref, back_ref, weight_ref, states, blocks, misfit, block_sems, other_sems,
):
    block_total = rows.shape[1]
    row_size = blocks.shape[0] // block_total
    members = back_ref.shape[1]
    state_total, _, col_size = states.shape
    chunk = block_total // CHUNKS

    back_copy = pltpu.make_async_copy(back_hbm, back_ref, other_sems.at[0])
    observed_copy = pltpu.make_async_copy(observed_hbm, misfit, other_sems.at[1])
    weight_copy = pltpu.make_async_copy(weight_hbm, weight_ref, other_sems.at[2])
    back_copy.start()
    observed_copy.start()
    for part in range(CHUNKS):
        span = pl.ds(part * chunk * row_size, chunk * row_size)
        pltpu.make_async_copy(blocks_hbm.at[span], blocks.at[span], block_sems.at[part]).start()
    weight_copy.start()

    back_copy.wait()
    for k in range(state_total):
        states[k] = back_ref[0, :, k * col_size:(k + 1) * col_size]
    out_ref[...] = jnp.zeros_like(out_ref)
    lane_half = lax.broadcasted_iota(jnp.int32, (members, 2 * row_size), 1) // row_size
    in_use = count[0]
    observed_copy.wait()

    def place(row):
        return pl.ds(pl.multiple_of(lax.shift_right_logical(row, 1) * (2 * row_size), 2 * row_size), 2 * row_size)

    batch = chunk // GROUP

    def tile_of(group):
        span = GROUP * row_size
        return blocks[pl.ds(pl.multiple_of(group * span, span), span), :]

    def apply_batch(part, _):
        pltpu.make_async_copy(
            blocks_hbm.at[pl.ds(0, chunk * row_size)],
            blocks.at[pl.ds(0, chunk * row_size)],
            block_sems.at[part],
        ).wait()
        results = []
        for g in range(batch):
            first = part * chunk + g * GROUP
            picked = jnp.concatenate([states[cols[0, first + j]] for j in range(GROUP)], axis=0)
            results.append(lax.dot_general(
                picked, tile_of(part * batch + g), (((1,), (1,)), ((), ())),
                preferred_element_type=jnp.float32,
            ))
        for g in range(batch):
            first = part * chunk + g * GROUP
            for j in range(GROUP):
                row = rows[0, first + j]
                half = row & 1
                piece = results[g][
                    j * members:(j + 1) * members,
                    (j // 2) * 2 * row_size:(j // 2 + 1) * 2 * row_size,
                ]
                piece = pltpu.roll(piece, (half ^ (j % 2)) * row_size, 1)
                wanted = jnp.where(first + j < in_use, half, 2)
                at = place(row)
                misfit[:, at] = misfit[:, at] - jnp.where(lane_half == wanted, piece, 0.0)
        return 0

    lax.fori_loop(0, CHUNKS, apply_batch, 0)
    weight_copy.wait()

    def pull_batch(part, _):
        results = []
        for g in range(batch):
            first = part * chunk + g * GROUP
            pieces = []
            for j in range(GROUP):
                row = rows[0, first + j]
                at = place(row)
                value = misfit[:, at] * weight_ref[:, at]
                value = pltpu.roll(value, ((row & 1) ^ (j % 2)) * row_size, 1)
                wanted = jnp.where(first + j < in_use, j % 2, 2)
                value = jnp.where(lane_half == wanted, value, 0.0).astype(jnp.bfloat16)
                nothing = jnp.zeros_like(value)
                pieces.append(jnp.concatenate(
                    [value if s == j // 2 else nothing for s in range(GROUP // 2)], axis=1
                ))
            results.append(jnp.dot(
                jnp.concatenate(pieces, axis=0), tile_of(part * batch + g),
                preferred_element_type=jnp.float32,
            ))
        for g in range(batch):
            first = part * chunk + g * GROUP
            for j in range(GROUP):
                k = cols[0, first + j]
                out_ref[k] = out_ref[k] + results[g][j * members:(j + 1) * members]
        return 0

    lax.fori_loop(0, CHUNKS, pull_batch, 0)


def gradients(obs_blocks, block_rows, block_cols, block_count, background, observed, obs_weight):
    _, block_total, row_size, col_size = obs_blocks.shape
    members = background.shape[1]
    state_total = background.shape[2] // col_size
    smem = pl.BlockSpec(memory_space=pltpu.SMEM)
    vmem = pl.BlockSpec(memory_space=pltpu.VMEM)
    hbm = pl.BlockSpec(memory_space=pltpu.HBM)
    return pl.pallas_call(
        gradient_kernel,
        out_shape=jax.ShapeDtypeStruct((state_total, members, col_size), jnp.float32),
        in_specs=[smem, smem, smem, hbm, hbm, hbm, hbm],
        out_specs=vmem,
        scratch_shapes=[
            pltpu.VMEM(background.shape, jnp.bfloat16),
            pltpu.VMEM(obs_weight.shape, jnp.float32),
            pltpu.VMEM((state_total, members, col_size), jnp.bfloat16),
            pltpu.VMEM((block_total * row_size, col_size), jnp.bfloat16),
            pltpu.VMEM((members, observed.shape[2]), jnp.float32),
            pltpu.SemaphoreType.DMA((CHUNKS,)),
            pltpu.SemaphoreType.DMA((3,)),
        ],
        compiler_params=pltpu.CompilerParams(vmem_limit_bytes=62 * 2**20),
        name="local_gradient",
    )(
        block_rows, block_cols, block_count, background, obs_weight,
        obs_blocks.reshape(block_total * row_size, col_size),
        observed.reshape(members, observed.shape[2]),
    )


def smoother_kernel(
    n, grad_ref, info_ref, decay_ref, noise_ref, prior_ref, out,
    coef_send, coef_recv, grad_recv, mean_send, var_send,
    coef_ss, coef_rs, grad_ss, grad_rs, mean_ss, mean_rs, var_ss, var_rs, own_sems,
):
    me = lax.axis_index("tm")
    width = coef_send.shape[2]
    members = mean_send.shape[1]

    barrier = pltpu.get_barrier_semaphore()

    def greet(d, _):
        pl.semaphore_signal(
            barrier, inc=1, device_id={"tm": lax.rem(me + d, n)}, device_id_type=MESH
        )
        return 0

    lax.fori_loop(1, n, greet, 0)
    own_grad = pltpu.make_async_copy(grad_ref.at[me], grad_recv.at[me], own_sems.at[0])
    own_grad.start()
    for k in range(n):
        columns = slice(k * width, (k + 1) * width)
        coef_send[k] = jnp.concatenate(
            [info_ref[:, columns], decay_ref[:, columns], noise_ref[:, columns],
             jnp.zeros((1, width), jnp.float32)], axis=0
        )
    mine = pl.ds(pl.multiple_of(me * width, width), width)
    coef_recv[me] = coef_send[me]
    pl.semaphore_wait(barrier, n - 1)

    def start_all(src, dst, send_sem, recv_sem):
        def body(i, _):
            d = n // 2 + i
            to = lax.rem(me + jnp.where(d < n, d, d - n + 1), n)
            pltpu.make_async_remote_copy(
                src_ref=src.at[to], dst_ref=dst(me), send_sem=send_sem, recv_sem=recv_sem,
                device_id={"tm": to}, device_id_type=MESH,
            ).start()
            return 0
        lax.fori_loop(0, n - 1, body, 0)

    def everything(src, whole, send_sem, recv_sem):
        return pltpu.make_async_remote_copy(
            src_ref=src.at[pl.ds(0, n - 1)], dst_ref=whole, send_sem=send_sem, recv_sem=recv_sem,
            device_id={"tm": lax.rem(me + 1, n)}, device_id_type=MESH,
        )

    def columns_of(first, last):
        return lambda k: out.at[
            first:last, pl.ds(pl.multiple_of(k * width, width), width)
        ]

    start_all(coef_send, lambda k: coef_recv.at[k], coef_ss, coef_rs)
    start_all(grad_ref, lambda k: grad_recv.at[k], grad_ss, grad_rs)
    others = pl.ds(0, (n - 1) * width)
    coefs = everything(coef_send, coef_recv.at[pl.ds(0, n - 1)], coef_ss, coef_rs)
    grads = everything(grad_ref, grad_recv.at[pl.ds(0, n - 1)], grad_ss, grad_rs)
    means = everything(mean_send, out.at[0:members, others], mean_ss, mean_rs)
    varis = everything(var_send, out.at[members:members + 1, others], var_ss, var_rs)
    coefs.wait_recv()

    info = [coef_recv[t, 0:1, :] for t in range(n)]
    decay = [coef_recv[t, 1:2, :] for t in range(n)]
    noise = [coef_recv[t, 2:3, :] for t in range(n)]
    var, carry = [], []
    for t in range(n):
        if t == 0:
            pred = prior_ref[:, mine]
            carry.append(None)
        else:
            pred = decay[t] * decay[t] * var[t - 1] + noise[t]
        scale = 1.0 / (1.0 + info[t] * pred)
        var.append(pred * scale)
        if t > 0:
            carry.append(scale * decay[t])
    gain = []
    later = [None] * n
    later[n - 1] = var[n - 1]
    for t in range(n - 1):
        pred = decay[t + 1] * decay[t + 1] * var[t] + noise[t + 1]
        gain.append(var[t] * decay[t + 1] / pred)
    for t in range(n - 2, -1, -1):
        pred = decay[t + 1] * decay[t + 1] * var[t] + noise[t + 1]
        later[t] = var[t] + gain[t] * gain[t] * (later[t + 1] - pred)
    for t in range(n):
        var_send[t] = later[t]
    start_all(var_send, columns_of(members, members + 1), var_ss, var_rs)
    own_var = pltpu.make_async_copy(
        var_send.at[me], columns_of(members, members + 1)(me), own_sems.at[1]
    )
    own_var.start()

    own_grad.wait()
    grads.wait_recv()
    mean = []
    for t in range(n):
        now = var[t] * grad_recv[t]
        mean.append(now if t == 0 else carry[t] * mean[t - 1] + now)
    smooth = mean[n - 1]
    mean_send[n - 1] = smooth
    for t in range(n - 2, -1, -1):
        smooth = mean[t] + gain[t] * (smooth - decay[t + 1] * mean[t])
        mean_send[t] = smooth
    start_all(mean_send, columns_of(0, members), mean_ss, mean_rs)
    own_mean = pltpu.make_async_copy(mean_send.at[me], columns_of(0, members)(me), own_sems.at[2])
    own_mean.start()

    own_var.wait()
    own_mean.wait()
    varis.wait_recv()
    means.wait_recv()
    coefs.wait_send()
    grads.wait_send()
    varis.wait_send()
    means.wait_send()


def split_kernel(both, mean_out, var_out, sems):
    members = mean_out.shape[1]
    mean_copy = pltpu.make_async_copy(both.at[0:members], mean_out.at[0], sems.at[0])
    var_copy = pltpu.make_async_copy(both.at[members:members + 1], var_out, sems.at[1])
    mean_copy.start()
    var_copy.start()
    mean_copy.wait()
    var_copy.wait()


def exchange_and_smooth(n, gradient, info_diag, decay, noise_var, prior_var):
    state_total, members, width = gradient.shape
    total = state_total * width
    vmem = pl.BlockSpec(memory_space=pltpu.VMEM)
    hbm = pl.BlockSpec(memory_space=pltpu.HBM)
    out = pl.pallas_call(
        functools.partial(smoother_kernel, n),
        out_shape=jax.ShapeDtypeStruct((members + 1, total), jnp.float32),
        in_specs=[hbm] + [vmem] * 4,
        out_specs=pl.BlockSpec(memory_space=pl.ANY),
        scratch_shapes=[
            pltpu.VMEM((n, 4, width), jnp.float32),
            pltpu.VMEM((n, 4, width), jnp.float32),
            pltpu.VMEM((n, members, width), jnp.float32),
            pltpu.VMEM((n, members, width), jnp.float32),
            pltpu.VMEM((n, 1, width), jnp.float32),
        ] + [pltpu.SemaphoreType.DMA] * 8 + [pltpu.SemaphoreType.DMA((3,))],
        compiler_params=pltpu.CompilerParams(collective_id=0, has_side_effects=True, vmem_limit_bytes=8 * 2**20),
        name="exchange_smooth",
    )(gradient, info_diag, decay, noise_var, prior_var.reshape(1, total))
    return pl.pallas_call(
        split_kernel,
        out_shape=(
            jax.ShapeDtypeStruct((1, members, total), jnp.float32),
            jax.ShapeDtypeStruct((1, total), jnp.float32),
        ),
        in_specs=[pl.BlockSpec(memory_space=pl.ANY)],
        out_specs=(hbm, hbm),
        scratch_shapes=[pltpu.SemaphoreType.DMA((2,))],
        compiler_params=pltpu.CompilerParams(vmem_limit_bytes=8 * 2**20),
        name="split_outputs",
    )(out)


def sequential_smoother(series, prior_here, member_total):
    full_steps = series.shape[0]
    grad_all = series[:, :member_total, :]
    info_all = series[:, member_total, :]
    decay_all = series[:, member_total + 1, :]
    noise_all = series[:, member_total + 2, :]
    local_width = series.shape[2]
    step_ids = jnp.arange(full_steps)
    first_flags = step_ids == 0
    final_flags = step_ids == full_steps - 1

    def forward(carried, inputs):
        mean_prev, var_prev = carried
        grad_now, info_now, decay_now, noise_now, first_now = inputs
        pred_var = jnp.where(first_now, prior_here, decay_now * decay_now * var_prev + noise_now)
        pred_mean = jnp.where(first_now, 0.0, decay_now * mean_prev)
        var_now = pred_var / (1.0 + info_now * pred_var)
        mean_now = var_now * (pred_mean / pred_var + grad_now)
        return ((mean_now, var_now), (mean_now, var_now))

    initial = (
        jnp.zeros((member_total, local_width), jnp.float32),
        jnp.ones((local_width,), jnp.float32),
    )
    means, variances = lax.scan(
        forward, initial, (grad_all, info_all, decay_all, noise_all, first_flags)
    )[1]
    next_decay = jnp.concatenate([decay_all[1:], jnp.zeros((1, local_width), jnp.float32)], axis=0)
    next_noise = jnp.concatenate([noise_all[1:], jnp.ones((1, local_width), jnp.float32)], axis=0)

    def backward(carried, inputs):
        later_mean, later_var = carried
        mean_now, var_now, decay_next, noise_next, final_now = inputs
        pred_var = decay_next * decay_next * var_now + noise_next
        smoother_gain = jnp.where(final_now, 0.0, var_now * decay_next / pred_var)
        out_mean = mean_now + smoother_gain * (later_mean - decay_next * mean_now)
        out_var = var_now + smoother_gain * smoother_gain * (later_var - pred_var)
        return ((out_mean, out_var), (out_mean, out_var))

    closing = (
        jnp.zeros((member_total, local_width), jnp.float32),
        jnp.zeros((local_width,), jnp.float32),
    )
    return lax.scan(
        backward, closing, (means, variances, next_decay, next_noise, final_flags), reverse=True
    )[1]


def shards(
    obs_blocks,
    block_rows,
    block_cols,
    block_count,
    background,
    observed,
    obs_weight,
    info_diag,
    decay,
    noise_var,
    prior_var,
):
    member_total = background.shape[1]
    state_total = background.shape[2]
    n = lax.axis_size("tm")
    gradient = gradients(
        obs_blocks, block_rows, block_cols, block_count, background, observed, obs_weight
    )
    local_width = state_total // n
    if local_width == gradient.shape[2]:
        return exchange_and_smooth(n, gradient, info_diag, decay, noise_var, prior_var)
    gradient = jnp.transpose(gradient, (1, 0, 2)).reshape(1, member_total, state_total)
    packed = jnp.concatenate(
        [gradient, info_diag[:, None, :], decay[:, None, :], noise_var[:, None, :]], axis=1
    )
    series = lax.all_to_all(packed, "tm", split_axis=2, concat_axis=0, tiled=True)
    prior_here = lax.dynamic_slice_in_dim(
        prior_var, lax.axis_index("tm") * local_width, local_width, 0
    )
    mean_series, var_series = sequential_smoother(series, prior_here, member_total)
    outgoing = jnp.concatenate([mean_series, var_series[:, None, :]], axis=1)
    returned = lax.all_to_all(outgoing, "tm", split_axis=0, concat_axis=2, tiled=True)
    return (returned[:, :member_total, :], returned[:, member_total, :])


def solution(mesh):
    in_specs = (
        P(("group", "tm"), None, None, None),
        P(("group", "tm"), None),
        P(("group", "tm"), None),
        P(("group", "tm")),
        P(("group", "tm"), None, None),
        P(("group", "tm"), None, None),
        P(("group", "tm"), None),
        P(("group", "tm"), None),
        P(("group", "tm"), None),
        P(("group", "tm"), None),
        P("group"),
    )
    out_specs = (P(("group", "tm"), None, None), P(("group", "tm"), None))
    return jax.shard_map(shards, mesh=mesh, in_specs=in_specs, out_specs=out_specs, check_vma=False)
```

time: 48.9 us -> 31.7 us (0.65)
  Pallas kernels: 44.5 us -> 29.2 us
  local copies, waits for them, and re-layouts: 2.86 us -> 0.92 us
    pallas_call x1, Pallas kernels: 25.2 us -> 11.2 us  [gradients(): pl.pallas_call(gradient_kernel, out_shape=jax.ShapeDtypeStruct((state_tot...]
    unnamed x2 -> x10, local copies, waits for them, and re-layouts: 2.86 us -> 0.92 us
    pallas_call x1 -> x2, Pallas kernels: 19.3 us -> 17.9 us  [the longest x1 17.3 us: exchange_and_smooth(): pl.pallas_call(functools.partial(smoother_kernel, n), out_shape=jax.Shape...]
where the time goes in v2:
time: 31.7 us; the launch traced here: 31.5 us
  Pallas kernels  29.2 us (92%)
  between operations  1.4 us (4%)
  local copies, waits for them, and re-layouts  0.92 us (3%)
    pallas_call x1, Pallas kernels, exchange_and_smooth(): pl.pallas_call(functools.partial(smoother_kernel, n), out_shape=jax.Shape...  17.3 us
    pallas_call x1, Pallas kernels, gradients(): pl.pallas_call(gradient_kernel, out_shape=jax.ShapeDtypeStruct((state_tot...  11.2 us
    unnamed x10, local copies, waits for them, and re-layouts  0.92 us
    pallas_call x1, Pallas kernels, exchange_and_smooth(): pl.pallas_call(split_kernel, out_shape=(jax.ShapeDtypeStruct((1, members,...  0.68 us

profile of v2, /device:TPU:0, one launch (start us, length us, event | category | flops | bytes accessed | tf_op | source)
XLA Modules:
  0.0 31.5 jit_solution(10859043574078009474)
XLA Ops:
  0.6 0.0 copy-start.4
  0.6 0.0 copy-start.3
  0.7 0.0 copy-start.2
  0.7 0.0 copy-start.1
  1.3 11.2 %local_gradient.1.grad_ref = f32[16,16,128]{2,1,0:T(8,128)} custom-call(s32[1,512]{1,0:T(1,128)} %rows.1, s32[1,512]{1,0:T(1,128)} %cols.1, s32[1]{0:T(128)S(6)} %copy.13.count, bf16[1,16,2048]{2,1,0:T(8,128)(2,1)} %back_hbm.1, f32[1,32768]{1,0:T(1,128)} %weight_hbm.1, bf16[32768,128]{1,0:T(8,128)(2,1)} %bitcast.4, f32[16,32768]{1,0:T(8,128)} %bitcast.5), custom_call_target="tpu_custom_call" | custom-call | tf_op jit(solution)/shard_map/local_gradient/pallas_call | solution.py:121
  12.6 0.0 copy-done.4
  12.6 0.0 copy-done.3
  12.6 0.0 copy-done.2
  12.6 0.0 copy-done.1
  12.6 0.0 copy-start
  12.7 0.9 %copy-done = f32[16,16,128]{2,1,0:T(8,128)S(1)} copy-done((f32[16,16,128]{2,1,0:T(8,128)S(1)}, f32[16,16,128]{2,1,0:T(8,128)}, u32[]{:S(2)}) %copy-start) | copy-done | bytes 131096
  13.5 17.3 %exchange_smooth.1.both = f32[17,2048]{1,0:T(8,128)S(1)} custom-call(f32[16,16,128]{2,1,0:T(8,128)S(1)} %copy-done, f32[1,2048]{1,0:T(1,128)S(1)} %copy-done.1, f32[1,2048]{1,0:T(1,128)S(1)} %copy-done.2, f32[1,2048]{1,0:T(1,128)S(1)} %copy-done.3, f32[1,2048]{1,0:T(1,128)S(1)} %bitcast.3), custom_call_target="tpu_custom_call" | custom-call | tf_op jit(solution)/shard_map/exchange_smooth/pallas_call | solution.py:276
  30.8 0.7 %split_outputs.1 = (f32[1,16,2048]{2,1,0:T(8,128)}, f32[1,2048]{1,0:T(1,128)}) custom-call(f32[17,2048]{1,0:T(8,128)S(1)} %exchange_smooth.1.both), custom_call_target="tpu_custom_call" | custom-call | tf_op jit(solution)/shard_map/split_outputs/pallas_call | solution.py:291
Async XLA Ops:
  0.6 12.0 %copy-start.4 = (f32[2048]{0:T(1024)S(1)}, f32[2048]{0:T(1024)}, u32[]{:S(2)}) copy-start(f32[2048]{0:T(1024)} %param.21) | copy-start | bytes 24580
  0.6 12.0 %copy-start.3 = (f32[1,2048]{1,0:T(1,128)S(1)}, f32[1,2048]{1,0:T(1,128)}, u32[]{:S(2)}) copy-start(f32[1,2048]{1,0:T(1,128)} %noise_ref.1) | copy-start | bytes 24580
  0.7 12.0 %copy-start.2 = (f32[1,2048]{1,0:T(1,128)S(1)}, f32[1,2048]{1,0:T(1,128)}, u32[]{:S(2)}) copy-start(f32[1,2048]{1,0:T(1,128)} %decay_ref.1) | copy-start | bytes 24580
  0.7 12.0 %copy-start.1 = (f32[1,2048]{1,0:T(1,128)S(1)}, f32[1,2048]{1,0:T(1,128)}, u32[]{:S(2)}) copy-start(f32[1,2048]{1,0:T(1,128)} %info_ref.1) | copy-start | bytes 24580
  12.6 0.9 %copy-start = (f32[16,16,128]{2,1,0:T(8,128)S(1)}, f32[16,16,128]{2,1,0:T(8,128)}, u32[]{:S(2)}) copy-start(f32[16,16,128]{2,1,0:T(8,128)} %local_gradient.1.grad_ref) | copy-start | bytes 393220

commit v3 on v2

--- a/solution.py
+++ b/solution.py
@@ -180,7 +180,7 @@
                 device_id={"tm": to}, device_id_type=MESH,
             ).start()
             return 0
-        lax.fori_loop(0, n - 1, body, 0)
+        lax.fori_loop(0, n - 1, body, 0, unroll=5)
 
     def everything(src, whole, send_sem, recv_sem):
         return pltpu.make_async_remote_copy(

time: 31.7 us -> 31.7 us (level)
  no operation moved by 1% of the time
where the time goes in v3:
time: 31.7 us; the launch traced here: 31.4 us
  Pallas kernels  29.1 us (92%)
  between operations  1.4 us (4%)
  local copies, waits for them, and re-layouts  0.92 us (3%)
    pallas_call x1, Pallas kernels, exchange_and_smooth(): pl.pallas_call(functools.partial(smoother_kernel, n), out_shape=jax.Shape...  17.2 us
    pallas_call x1, Pallas kernels, gradients(): pl.pallas_call(gradient_kernel, out_shape=jax.ShapeDtypeStruct((state_tot...  11.2 us
    unnamed x10, local copies, waits for them, and re-layouts  0.92 us
    pallas_call x1, Pallas kernels, exchange_and_smooth(): pl.pallas_call(split_kernel, out_shape=(jax.ShapeDtypeStruct((1, members,...  0.68 us

profile of v3, /device:TPU:0, one launch (start us, length us, event | category | flops | bytes accessed | tf_op | source)
XLA Modules:
  0.0 31.4 jit_solution(4326393321592544142)
XLA Ops:
  0.6 0.0 copy-start.4
  0.6 0.0 copy-start.3
  0.7 0.0 copy-start.2
  0.7 0.0 copy-start.1
  1.3 11.2 %local_gradient.1.grad_ref = f32[16,16,128]{2,1,0:T(8,128)} custom-call(s32[1,512]{1,0:T(1,128)} %rows.1, s32[1,512]{1,0:T(1,128)} %cols.1, s32[1]{0:T(128)S(6)} %copy.13.count, bf16[1,16,2048]{2,1,0:T(8,128)(2,1)} %back_hbm.1, f32[1,32768]{1,0:T(1,128)} %weight_hbm.1, bf16[32768,128]{1,0:T(8,128)(2,1)} %bitcast.4, f32[16,32768]{1,0:T(8,128)} %bitcast.5), custom_call_target="tpu_custom_call" | custom-call | tf_op jit(solution)/shard_map/local_gradient/pallas_call | solution.py:121
  12.6 0.0 copy-done.4
  12.6 0.0 copy-done.3
  12.6 0.0 copy-done.2
  12.6 0.0 copy-done.1
  12.6 0.0 copy-start
  12.7 0.9 %copy-done = f32[16,16,128]{2,1,0:T(8,128)S(1)} copy-done((f32[16,16,128]{2,1,0:T(8,128)S(1)}, f32[16,16,128]{2,1,0:T(8,128)}, u32[]{:S(2)}) %copy-start) | copy-done | bytes 131096
  13.6 17.2 %exchange_smooth.1.both = f32[17,2048]{1,0:T(8,128)S(1)} custom-call(f32[16,16,128]{2,1,0:T(8,128)S(1)} %copy-done, f32[1,2048]{1,0:T(1,128)S(1)} %copy-done.1, f32[1,2048]{1,0:T(1,128)S(1)} %copy-done.2, f32[1,2048]{1,0:T(1,128)S(1)} %copy-done.3, f32[1,2048]{1,0:T(1,128)S(1)} %bitcast.3), custom_call_target="tpu_custom_call" | custom-call | tf_op jit(solution)/shard_map/exchange_smooth/pallas_call | solution.py:276
  30.8 0.7 %split_outputs.1 = (f32[1,16,2048]{2,1,0:T(8,128)}, f32[1,2048]{1,0:T(1,128)}) custom-call(f32[17,2048]{1,0:T(8,128)S(1)} %exchange_smooth.1.both), custom_call_target="tpu_custom_call" | custom-call | tf_op jit(solution)/shard_map/split_outputs/pallas_call | solution.py:291
Async XLA Ops:
  0.6 12.0 %copy-start.4 = (f32[2048]{0:T(1024)S(1)}, f32[2048]{0:T(1024)}, u32[]{:S(2)}) copy-start(f32[2048]{0:T(1024)} %param.21) | copy-start | bytes 24580
  0.6 12.0 %copy-start.3 = (f32[1,2048]{1,0:T(1,128)S(1)}, f32[1,2048]{1,0:T(1,128)}, u32[]{:S(2)}) copy-start(f32[1,2048]{1,0:T(1,128)} %noise_ref.1) | copy-start | bytes 24580
  0.7 12.0 %copy-start.2 = (f32[1,2048]{1,0:T(1,128)S(1)}, f32[1,2048]{1,0:T(1,128)}, u32[]{:S(2)}) copy-start(f32[1,2048]{1,0:T(1,128)} %decay_ref.1) | copy-start | bytes 24580
  0.7 12.0 %copy-start.1 = (f32[1,2048]{1,0:T(1,128)S(1)}, f32[1,2048]{1,0:T(1,128)}, u32[]{:S(2)}) copy-start(f32[1,2048]{1,0:T(1,128)} %info_ref.1) | copy-start | bytes 24580
  12.6 0.9 %copy-start = (f32[16,16,128]{2,1,0:T(8,128)S(1)}, f32[16,16,128]{2,1,0:T(8,128)}, u32[]{:S(2)}) copy-start(f32[16,16,128]{2,1,0:T(8,128)} %local_gradient.1.grad_ref) | copy-start | bytes 393220
